TPU v7x, 32 devices: a whole 2x2x4 slice. The times are simulated.
32 devices in a mesh: rows: 16 (over z, y, core), rep: 2 (over x).
Axes of the slice: x: 2, y: 2, z: 4, core: 2. Of those that a mesh axis runs over, the one named last changes fastest.
Arguments:
- embeddings: bfloat16 [11264, 1024], P(('rows', 'rep')), may hold values from -6 to 6
- owner_ids: int32 [11264, 1], P(('rows', 'rep')), may hold values from 0 to 15; in each aligned block of 352 rows (0 to 351, 352 to 703, ...) at most 64 rows name the same one
- live_mask: int32 [11264], P(('rows', 'rep')), may hold values 0 or 1
Outputs:
- neighbour_means: bfloat16 [11264, 1024], P(('rows', 'rep'))
Inputs may be any that keep to these rules, and one draw needn't show every extreme that they name: `owner_ids`: among the rows of one device, at most 64 name the same owner, and in every draw some owner is named by exactly 64 of them.
All inputs are finite; a program needn't handle non-finite values. Where the computation divides by a largest or mean magnitude, that divisor is 1e-20 or more. No bound on the sum of `live_mask` on one device may be relied on, other than what follows from the above.
Results may differ from a plain program's by a relative error of at most 0.0017.
The roundings to bfloat16 on the way count: a program that leaves them out, or rounds other values in their place, can miss the bound.
Values may be sent and summed in bfloat16 or wider, within the bound.
A program may use at most 64 MiB of HBM per device.

v0:
```python
import jax
import jax.numpy as jnp
from jax import lax
from jax.sharding import PartitionSpec as P

BUCKET = 1024
KERNEL_SCALE = 4.0
EPSILON = 1e-06
PRECISE = lax.Precision.HIGHEST


def block_positions(owner_block, owners, slot_cap):
    onehot = (owner_block[:, None] == jnp.arange(owners, dtype=jnp.int32)[None, :]).astype(
        jnp.int32
    )
    before = jnp.cumsum(onehot, axis=0) - onehot
    slot_rank = jnp.sum(before * onehot, axis=1)
    return owner_block * slot_cap + slot_rank


def whiten(embedded, inverse_root):
    mapped = jnp.dot(embedded, inverse_root, preferred_element_type=jnp.float32)
    return (mapped * lax.rsqrt(jnp.mean(mapped * mapped, axis=1, keepdims=True) + EPSILON)).astype(
        jnp.bfloat16
    )


def bucket_means(members, alive):
    scores = jnp.dot(members, members.T, preferred_element_type=jnp.float32)
    weights = jnp.exp(KERNEL_SCALE * (scores / members.shape[1] - 1.0)) * alive[None, :]
    denominator = jnp.sum(weights, axis=1, keepdims=True)
    summed = jnp.dot(weights.astype(jnp.bfloat16), members, preferred_element_type=jnp.float32)
    averaged = summed / jnp.where(alive[:, None] > 0, denominator, 1.0)
    normed = averaged * lax.rsqrt(jnp.mean(averaged * averaged, axis=1, keepdims=True) + EPSILON)
    return (normed * alive[:, None]).astype(jnp.bfloat16)


def spread(values, positions, slots_all):
    return jnp.zeros((slots_all,) + values.shape[1:], values.dtype).at[positions].set(values)


def first_rows(start_y, first_row, row_share):
    y_rows = lax.dynamic_slice_in_dim(start_y, first_row, row_share, 0)
    return 0.5 * (3.0 * y_rows - jnp.dot(y_rows, start_y, precision=PRECISE))


def second_rows(next_y, next_z, first_row, row_share):
    z_rows = lax.dynamic_slice_in_dim(next_z, first_row, row_share, 0)
    product = jnp.dot(z_rows, next_y, precision=PRECISE)
    return 0.5 * (3.0 * z_rows - jnp.dot(product, next_z, precision=PRECISE))


def per_device(embeddings, owner_ids, live_mask):
    rows_here, columns = embeddings.shape
    owners = lax.axis_size("rows")
    slot_cap = BUCKET // owners
    positions = block_positions(owner_ids[:, 0], owners, slot_cap)
    live_rows = live_mask.astype(jnp.bfloat16)
    masked = embeddings * live_rows[:, None]
    partial_moment = lax.dot_general(
        masked, masked, (((0,), (0,)), ((), ())), preferred_element_type=jnp.float32
    )
    moment = lax.psum(partial_moment, ("rows", "rep"))
    start_y = moment / jnp.max(jnp.sum(jnp.abs(moment), axis=1))
    next_z = 0.5 * (3.0 * jnp.eye(columns, dtype=jnp.float32) - start_y)
    row_share = columns // lax.axis_size("rep")
    first_row = lax.axis_index("rep") * row_share
    next_y = lax.all_gather(first_rows(start_y, first_row, row_share), "rep", axis=0, tiled=True)
    inverse_root = lax.all_gather(
        second_rows(next_y, next_z, first_row, row_share).astype(jnp.bfloat16),
        "rep",
        axis=0,
        tiled=True,
    )
    whitened = whiten(embeddings, inverse_root)
    sent_rows, sent_live = (
        lax.all_to_all(
            spread(whitened, positions, BUCKET).reshape(owners, slot_cap, columns),
            "rows",
            split_axis=0,
            concat_axis=0,
            tiled=True,
        ),
        lax.all_to_all(
            spread(live_rows, positions, BUCKET).reshape(owners, slot_cap),
            "rows",
            split_axis=0,
            concat_axis=0,
            tiled=True,
        ),
    )
    members = sent_rows.reshape(BUCKET, columns)
    member_live = sent_live.reshape(BUCKET).astype(jnp.float32)
    means = bucket_means(members, member_live)
    returned = lax.all_to_all(
        means.reshape(owners, slot_cap, columns), "rows", split_axis=0, concat_axis=0, tiled=True
    )
    return returned.reshape(BUCKET, columns)[positions]


def solution(mesh):
    placed = (P(("rows", "rep"), None), P(("rows", "rep"), None), P(("rows", "rep")))
    return jax.shard_map(
        per_device, mesh=mesh, in_specs=placed, out_specs=P(("rows", "rep"), None), check_vma=False
    )
```

profile of v0, /device:TPU:13, one launch (start us, length us, event | category | flops | bytes accessed | tf_op | source)
XLA Modules:
  0.0 409.3 jit_solution(2860625432853445525)
XLA Ops:
  6.5 0.7 convert_element_type.41
  7.2 4.6 %fusion.21 = f32[1024,1024]{1,0:T(8,128)} fusion(bf16[352,1024]{1,0:T(8,128)(2,1)} %param.3, bf16[352]{0:T(512)(128)(2,1)S(1)} %convert_element_type.41), kind=kOutput, calls=%fused_computation.30 | convolution fusion | flops 738557952 | bytes 4915904 | tf_op jit(solution)/shard_map/dot_general | solution.py:60
  11.9 0.0 all-reduce.3.cloned.1.call-update
  11.9 0.0 all-gather.3.cloned.1.call-start
  11.9 141.8 %all-reduce.3.cloned.1.call-done = f32[1024,1024]{1,0:T(8,128)} async-done(((f32[1024,1024]{1,0:T(8,128)}), f32[1024,1024]{1,0:T(8,128)}) %all-reduce.3.cloned.1.call-update) | async-done | bytes 4194320 | tf_op jit(solution)/shard_map/psum | solution.py:63
  153.8 2.6 abs_reduce_fusion
  156.3 0.6 reduce_max.9
  156.9 5.7 %subtract_multiply_fusion = (f32[1024,1024]{1,0:T(8,128)}, f32[1024,1024]{1,0:T(8,128)S(1)}) fusion(f32[1024,1024]{1,0:T(8,128)} %all-reduce.3.cloned.1.call-done, f32[]{:T(128)} %reduce_max.9), kind=kLoop, calls=%fused_computation.6 | loop fusion | flops 5242880 | bytes 12582916 | tf_op jit(solution)/shard_map/mul | solution.py:65
  162.7 8.4 %subtract_multiply_fusion.1 = f32[512,1024]{1,0:T(8,128)} fusion(f32[1024,1024]{1,0:T(8,128)S(1)} %get-tuple-element.6, s32[]{:T(128)S(6)} %select_n.20), kind=kOutput, calls=%fused_computation.18 | convolution fusion | flops 6444023808 | bytes 10486784 | tf_op jit(solution)/shard_map/dot_general | solution.py:44
  171.1 0.0 all-gather.3.cloned.1.call-update
  171.1 0.2 all-gather.5.cloned.1.call-start
  171.3 57.7 %all-gather.3.cloned.1.call-done = f32[1024,1024]{1,0:T(8,128)} async-done(((f32[512,1024]{1,0:T(8,128)}), f32[1024,1024]{1,0:T(8,128)}) %all-gather.3.cloned.1.call-update) | async-done | bytes 4194320 | tf_op jit(solution)/shard_map/all_gather | solution.py:68
  229.0 10.0 %fusion.10 = f32[512,1024]{1,0:T(8,128)S(1)} fusion(f32[1024,1024]{1,0:T(8,128)} %all-gather.3.cloned.1.call-done, f32[1024,1024]{1,0:T(8,128)} %get-tuple-element.5, s32[]{:T(128)S(6)} %select_n.20), kind=kOutput, calls=%fused_computation.22 | convolution fusion | flops 6442450944 | bytes 8388612 | tf_op jit(solution)/shard_map/dot_general | solution.py:49
  239.1 8.0 %multiply_convert_fusion.1 = bf16[512,1024]{1,0:T(8,128)(2,1)} fusion(f32[1024,1024]{1,0:T(8,128)S(1)} %copy-done, s32[]{:T(128)S(6)} %select_n.20, f32[512,1024]{1,0:T(8,128)S(1)} %fusion.10), kind=kOutput, calls=%fused_computation.17 | convolution fusion | flops 6444548096 | bytes 9437188 | tf_op jit(solution)/shard_map/dot_general | solution.py:50
  247.2 0.9 reduce-window.6
  248.1 0.2 slice_reduce_fusion
  248.3 0.1 bitcast_bitcast_fusion
  248.5 2.8 scatter_custom_fusion.1
  251.2 0.7 all_to_all.16
  251.9 6.4 %all-to-all-start.1 = ((bf16[16,1,64]{2,1,0:T(2,128)(2,1)}), bf16[16,1,64]{2,1,0:T(2,128)(2,1)S(1)}, u32[]{:S(2)}, u32[]{:S(2)}) async-start(bf16[16,1,64]{2,1,0:T(2,128)(2,1)} %all_to_all.16), calls=%async_computation.1 | async-start | bytes 16384 | tf_op jit(solution)/shard_map/all_to_all | solution.py:84
  258.3 22.1 %all-gather.5.cloned.1.call-done = bf16[1024,1024]{1,0:T(8,128)(2,1)} async-done(((bf16[512,1024]{1,0:T(8,128)(2,1)}), bf16[1024,1024]{1,0:T(8,128)(2,1)}) %all-gather.5.cloned.1.call-update) | async-done | bytes 2097168 | tf_op jit(solution)/shard_map/all_gather | solution.py:69
  280.4 2.6 multiply_reduce_fusion.1
  283.0 3.7 scatter_custom_fusion
  286.7 6.4 %all-to-all-start = ((bf16[16,64,1024]{2,1,0:T(8,128)(2,1)}), bf16[16,64,1024]{2,1,0:T(8,128)(2,1)S(1)}, u32[]{:S(2)}, u32[]{:S(2)}) async-start(bf16[16,64,1024]{2,1,0:T(8,128)(2,1)} %bitcast.2), calls=%async_computation | async-start | bytes 4194304 | tf_op jit(solution)/shard_map/all_to_all | solution.py:77
  293.1 0.1 reshape.77
  293.2 47.3 %all-to-all-done = bf16[16,64,1024]{2,1,0:T(8,128)(2,1)S(1)} async-done(((bf16[16,64,1024]{2,1,0:T(8,128)(2,1)}), bf16[16,64,1024]{2,1,0:T(8,128)(2,1)S(1)}, u32[]{:S(2)}, u32[]{:S(2)}) %all-to-all-start) | async-done | bytes 2097184 | tf_op jit(solution)/shard_map/all_to_all | solution.py:77
  340.5 2.7 fusion
  343.2 2.7 multiply_reduce_fusion
  346.0 1.8 multiply_convert_fusion
  347.8 4.9 %all-to-all-start.2 = ((bf16[16,64,1024]{2,1,0:T(8,128)(2,1)}), bf16[16,64,1024]{2,1,0:T(8,128)(2,1)S(1)}, u32[]{:S(2)}, u32[]{:S(2)}) async-start(bf16[16,64,1024]{2,1,0:T(8,128)(2,1)} %bitcast.30), calls=%async_computation.2 | async-start | bytes 4194304 | tf_op jit(solution)/shard_map/all_to_all | solution.py:95
  352.7 47.4 %all-to-all-done.2 = bf16[16,64,1024]{2,1,0:T(8,128)(2,1)S(1)} async-done(((bf16[16,64,1024]{2,1,0:T(8,128)(2,1)}), bf16[16,64,1024]{2,1,0:T(8,128)(2,1)S(1)}, u32[]{:S(2)}, u32[]{:S(2)}) %all-to-all-start.2) | async-done | bytes 2097184 | tf_op jit(solution)/shard_map/all_to_all | solution.py:95
  400.1 2.7 gather_fusion
  (20 shorter events, 0.2 us)
Async XLA Ops:
  6.5 147.2 %all-reduce.3.cloned.1.call-start = ((), (), s32[]{:S(2)}) async-start(), calls=%async_computation.3 | async-start | bytes 8388608 | tf_op jit(solution)/shard_map/psum | solution.py:63
  11.9 217.1 %all-gather.3.cloned.1.call-start = ((), (), s32[]{:S(2)}) async-start(), calls=%async_computation.4 | async-start | bytes 6291456 | tf_op jit(solution)/shard_map/all_gather | solution.py:68
  171.1 109.3 %all-gather.5.cloned.1.call-start = ((), (), s32[]{:S(2)}) async-start(), calls=%async_computation.5 | async-start | bytes 3145728 | tf_op jit(solution)/shard_map/all_gather | solution.py:69
  229.0 10.0 %copy-start = (f32[1024,1024]{1,0:T(8,128)S(1)}, f32[1024,1024]{1,0:T(8,128)}, u32[]{:S(2)}) copy-start(f32[1024,1024]{1,0:T(8,128)} %get-tuple-element.5) | copy-start | bytes 12582916
  239.0 8.1 %copy-start.2 = (s32[352,1]{0,1:T(1,128)S(1)}, s32[352,1]{0,1:T(1,128)}, u32[]{:S(2)}) copy-start(s32[352,1]{0,1:T(1,128)} %param.4) | copy-start | bytes 4228
  239.1 41.4 %copy-start.1 = (bf16[352,1024]{1,0:T(8,128)(2,1)S(1)}, bf16[352,1024]{1,0:T(8,128)(2,1)}, u32[]{:S(2)}) copy-start(bf16[352,1024]{1,0:T(8,128)(2,1)} %param.3) | copy-start | bytes 2162692
  251.9 34.8 %all-to-all-start.1 = ((bf16[16,1,64]{2,1,0:T(2,128)(2,1)}), bf16[16,1,64]{2,1,0:T(2,128)(2,1)S(1)}, u32[]{:S(2)}, u32[]{:S(2)}) async-start(bf16[16,1,64]{2,1,0:T(2,128)(2,1)} %all_to_all.16), calls=%async_computation.1 | async-start | bytes 16384 | tf_op jit(solution)/shard_map/all_to_all | solution.py:84
  286.7 53.8 %all-to-all-start = ((bf16[16,64,1024]{2,1,0:T(8,128)(2,1)}), bf16[16,64,1024]{2,1,0:T(8,128)(2,1)S(1)}, u32[]{:S(2)}, u32[]{:S(2)}) async-start(bf16[16,64,1024]{2,1,0:T(8,128)(2,1)} %bitcast.2), calls=%async_computation | async-start | bytes 4194304 | tf_op jit(solution)/shard_map/all_to_all | solution.py:77
  347.8 52.3 %all-to-all-start.2 = ((bf16[16,64,1024]{2,1,0:T(8,128)(2,1)}), bf16[16,64,1024]{2,1,0:T(8,128)(2,1)S(1)}, u32[]{:S(2)}, u32[]{:S(2)}) async-start(bf16[16,64,1024]{2,1,0:T(8,128)(2,1)} %bitcast.30), calls=%async_computation.2 | async-start | bytes 4194304 | tf_op jit(solution)/shard_map/all_to_all | solution.py:95
Sparse Core Ops, SparseCore 0:
  12.9 140.8 all-reduce.2
  171.2 57.7 all-gather.2
  247.3 33.1 all-gather.4
where the time goes:
time: 410 us; the launch traced here: 409 us
  waiting for transfers between devices  316 us (77%)
  matrix products  39.1 us (10%)
  starting transfers between devices  17.9 us (4%)
  other arithmetic  16.2 us (4%)
  between operations  13.2 us (3%)
  local copies, waits for them, and re-layouts  6.39 us (2%)
    psum x1, waiting for transfers between devices, per_device(): moment = lax.psum(partial_moment, ('rows', 'rep'))  142 us
    all_gather x1, waiting for transfers between devices, per_device(): lax.all_gather(first_rows(start_y, first_row, row_share), 'rep', axis=0,...  57.7 us
    all_to_all x1, waiting for transfers between devices, per_device(): lax.all_to_all(means.reshape(owners, slot_cap, columns), 'rows', split_ax...  47.4 us
    all_to_all x1, waiting for transfers between devices, per_device(): lax.all_to_all(spread(whitened, positions, BUCKET).reshape(owners, slot_c...  47.3 us
    all_gather x1, waiting for transfers between devices, per_device(): lax.all_gather(second_rows(next_y, next_z, first_row, row_share).astype(j...  22.1 us
    dot_general x1, matrix products, second_rows(): product = jnp.dot(z_rows, next_y, precision=PRECISE)  10 us
    dot_general x1, matrix products, first_rows(): return 0.5 * (3.0 * y_rows - jnp.dot(y_rows, start_y, precision=PRECISE))  8.4 us
  transfers between devices with their start and end apart: 6, of which 5 were waited for; matrix products, arithmetic and copies ran while one was open for 3% of the time, Pallas kernels for 0%

commit v1 on v0

--- a/solution.py
+++ b/solution.py
@@ -1,3 +1,4 @@
+import functools
 import jax
 import jax.numpy as jnp
 from jax import lax
@@ -7,6 +8,13 @@
 KERNEL_SCALE = 4.0
 EPSILON = 1e-06
 PRECISE = lax.Precision.HIGHEST
+
+
+def _handle_slots(block_here, net_axis, along_axis):
+    return jax.lax.psum(jax.lax.psum(block_here, net_axis), along_axis)
+
+
+_get_weights = functools.partial(_handle_slots, net_axis="rep", along_axis="rows")
 
 
 def block_positions(owner_block, owners, slot_cap):
@@ -60,7 +68,7 @@
     partial_moment = lax.dot_general(
         masked, masked, (((0,), (0,)), ((), ())), preferred_element_type=jnp.float32
     )
-    moment = lax.psum(partial_moment, ("rows", "rep"))
+    moment = _get_weights(partial_moment)
     start_y = moment / jnp.max(jnp.sum(jnp.abs(moment), axis=1))
     next_z = 0.5 * (3.0 * jnp.eye(columns, dtype=jnp.float32) - start_y)
     row_share = columns // lax.axis_size("rep")

time: 410 us -> 491 us (1.20)
  waiting for transfers between devices: 316 us -> 397 us
    psum x1 -> x2, waiting for transfers between devices: 142 us -> 223 us  [_handle_slots(): return jax.lax.psum(jax.lax.psum(block_here, net_axis), along_axis)]
  transfers between devices with their start and end apart: 6 -> 7, of which waited for: 5 -> 6; matrix products, arithmetic and copies ran while one was open for 3% -> 2% of each run, Pallas kernels for 0% -> 0%
where the time goes in v1:
time: 491 us; the launch traced here: 490 us
  waiting for transfers between devices  397 us (81%)
  matrix products  39.3 us (8%)
  starting transfers between devices  18 us (4%)
  other arithmetic  16.2 us (3%)
  between operations  13.2 us (3%)
  local copies, waits for them, and re-layouts  6.39 us (1%)
    psum x2, waiting for transfers between devices, _handle_slots(): return jax.lax.psum(jax.lax.psum(block_here, net_axis), along_axis)  223 us
    all_gather x1, waiting for transfers between devices, per_device(): lax.all_gather(first_rows(start_y, first_row, row_share), 'rep', axis=0,...  56.7 us
    all_to_all x1, waiting for transfers between devices, per_device(): lax.all_to_all(means.reshape(owners, slot_cap, columns), 'rows', split_ax...  47.4 us
    all_to_all x1, waiting for transfers between devices, per_device(): lax.all_to_all(spread(whitened, positions, BUCKET).reshape(owners, slot_c...  47.3 us
    all_gather x1, waiting for transfers between devices, per_device(): lax.all_gather(second_rows(next_y, next_z, first_row, row_share).astype(j...  22.1 us
    dot_general x1, matrix products, second_rows(): product = jnp.dot(z_rows, next_y, precision=PRECISE)  10 us
  transfers between devices with their start and end apart: 7, of which 6 were waited for; matrix products, arithmetic and copies ran while one was open for 2% of the time, Pallas kernels for 0%

profile of v1, /device:TPU:13, one launch (start us, length us, event | category | flops | bytes accessed | tf_op | source)
XLA Modules:
  0.0 490.1 jit_solution(3457433711483088804)
XLA Ops:
  6.5 0.7 convert_element_type.41
  7.2 4.8 fusion.21
  12.0 0.0 all-reduce.6.cloned.1.call-start
  12.1 109.1 %all-reduce.4.cloned.1.call-done = f32[1024,1024]{1,0:T(8,128)} async-done(((f32[1024,1024]{1,0:T(8,128)}), f32[1024,1024]{1,0:T(8,128)}) %all-reduce.4.cloned.1.call-update) | async-done | bytes 4194320 | tf_op jit(solution)/shard_map/psum | solution.py:14
  121.2 0.0 all-gather.3.cloned.1.call-start
  121.2 114.4 %all-reduce.6.cloned.1.call-done = f32[1024,1024]{1,0:T(8,128)} async-done(((f32[1024,1024]{1,0:T(8,128)}), f32[1024,1024]{1,0:T(8,128)}) %all-reduce.6.cloned.1.call-update) | async-done | bytes 4194320 | tf_op jit(solution)/shard_map/psum | solution.py:14
  235.6 2.6 abs_reduce_fusion
  238.2 0.6 reduce_max.9
  238.8 5.7 %subtract_multiply_fusion = (f32[1024,1024]{1,0:T(8,128)}, f32[1024,1024]{1,0:T(8,128)S(1)}) fusion(f32[1024,1024]{1,0:T(8,128)} %all-reduce.6.cloned.1.call-done, f32[]{:T(128)} %reduce_max.9), kind=kLoop, calls=%fused_computation.6 | loop fusion | flops 5242880 | bytes 12582916 | tf_op jit(solution)/shard_map/mul | solution.py:73
  244.5 8.4 %subtract_multiply_fusion.1 = f32[512,1024]{1,0:T(8,128)} fusion(f32[1024,1024]{1,0:T(8,128)S(1)} %get-tuple-element.6, s32[]{:T(128)S(6)} %select_n.20), kind=kOutput, calls=%fused_computation.18 | convolution fusion | flops 6444023808 | bytes 10486784 | tf_op jit(solution)/shard_map/dot_general | solution.py:52
  252.9 0.2 all-gather.5.cloned.1.call-start
  253.2 56.7 %all-gather.3.cloned.1.call-done = f32[1024,1024]{1,0:T(8,128)} async-done(((f32[512,1024]{1,0:T(8,128)}), f32[1024,1024]{1,0:T(8,128)}) %all-gather.3.cloned.1.call-update) | async-done | bytes 4194320 | tf_op jit(solution)/shard_map/all_gather | solution.py:76
  309.9 10.0 %fusion.10 = f32[512,1024]{1,0:T(8,128)S(1)} fusion(f32[1024,1024]{1,0:T(8,128)} %all-gather.3.cloned.1.call-done, f32[1024,1024]{1,0:T(8,128)} %get-tuple-element.5, s32[]{:T(128)S(6)} %select_n.20), kind=kOutput, calls=%fused_computation.22 | convolution fusion | flops 6442450944 | bytes 8388612 | tf_op jit(solution)/shard_map/dot_general | solution.py:57
  319.9 8.0 %multiply_convert_fusion.1 = bf16[512,1024]{1,0:T(8,128)(2,1)} fusion(f32[1024,1024]{1,0:T(8,128)S(1)} %copy-done, s32[]{:T(128)S(6)} %select_n.20, f32[512,1024]{1,0:T(8,128)S(1)} %fusion.10), kind=kOutput, calls=%fused_computation.17 | convolution fusion | flops 6444548096 | bytes 9437188 | tf_op jit(solution)/shard_map/dot_general | solution.py:58
  328.1 0.9 reduce-window.6
  328.9 0.2 slice_reduce_fusion
  329.2 0.1 bitcast_bitcast_fusion
  329.3 2.8 scatter_custom_fusion.1
  332.1 0.7 all_to_all.16
  332.8 6.4 %all-to-all-start.1 = ((bf16[16,1,64]{2,1,0:T(2,128)(2,1)}), bf16[16,1,64]{2,1,0:T(2,128)(2,1)S(1)}, u32[]{:S(2)}, u32[]{:S(2)}) async-start(bf16[16,1,64]{2,1,0:T(2,128)(2,1)} %all_to_all.16), calls=%async_computation.1 | async-start | bytes 16384 | tf_op jit(solution)/shard_map/all_to_all | solution.py:92
  339.1 22.1 %all-gather.5.cloned.1.call-done = bf16[1024,1024]{1,0:T(8,128)(2,1)} async-done(((bf16[512,1024]{1,0:T(8,128)(2,1)}), bf16[1024,1024]{1,0:T(8,128)(2,1)}) %all-gather.5.cloned.1.call-update) | async-done | bytes 2097168 | tf_op jit(solution)/shard_map/all_gather | solution.py:77
  361.3 2.6 multiply_reduce_fusion.1
  363.9 3.7 scatter_custom_fusion
  367.6 6.4 %all-to-all-start = ((bf16[16,64,1024]{2,1,0:T(8,128)(2,1)}), bf16[16,64,1024]{2,1,0:T(8,128)(2,1)S(1)}, u32[]{:S(2)}, u32[]{:S(2)}) async-start(bf16[16,64,1024]{2,1,0:T(8,128)(2,1)} %bitcast.2), calls=%async_computation | async-start | bytes 4194304 | tf_op jit(solution)/shard_map/all_to_all | solution.py:85
  374.0 0.1 reshape.77
  374.0 47.3 %all-to-all-done = bf16[16,64,1024]{2,1,0:T(8,128)(2,1)S(1)} async-done(((bf16[16,64,1024]{2,1,0:T(8,128)(2,1)}), bf16[16,64,1024]{2,1,0:T(8,128)(2,1)S(1)}, u32[]{:S(2)}, u32[]{:S(2)}) %all-to-all-start) | async-done | bytes 2097184 | tf_op jit(solution)/shard_map/all_to_all | solution.py:85
  421.4 2.7 fusion
  424.1 2.7 multiply_reduce_fusion
  426.8 1.8 multiply_convert_fusion
  428.6 4.9 %all-to-all-start.2 = ((bf16[16,64,1024]{2,1,0:T(8,128)(2,1)}), bf16[16,64,1024]{2,1,0:T(8,128)(2,1)S(1)}, u32[]{:S(2)}, u32[]{:S(2)}) async-start(bf16[16,64,1024]{2,1,0:T(8,128)(2,1)} %bitcast.30), calls=%async_computation.2 | async-start | bytes 4194304 | tf_op jit(solution)/shard_map/all_to_all | solution.py:103
  433.5 47.4 %all-to-all-done.2 = bf16[16,64,1024]{2,1,0:T(8,128)(2,1)S(1)} async-done(((bf16[16,64,1024]{2,1,0:T(8,128)(2,1)}), bf16[16,64,1024]{2,1,0:T(8,128)(2,1)S(1)}, u32[]{:S(2)}, u32[]{:S(2)}) %all-to-all-start.2) | async-done | bytes 2097184 | tf_op jit(solution)/shard_map/all_to_all | solution.py:103
  481.0 2.7 gather_fusion
  (23 shorter events, 0.3 us)
Async XLA Ops:
  6.5 114.6 %all-reduce.4.cloned.1.call-start = ((), (), s32[]{:S(2)}) async-start(), calls=%async_computation.3 | async-start | bytes 8388608 | tf_op jit(solution)/shard_map/psum | solution.py:14
  12.0 223.6 %all-reduce.6.cloned.1.call-start = ((), (), s32[]{:S(2)}) async-start(), calls=%async_computation.4 | async-start | bytes 8388608 | tf_op jit(solution)/shard_map/psum | solution.py:14
  121.2 188.7 %all-gather.3.cloned.1.call-start = ((), (), s32[]{:S(2)}) async-start(), calls=%async_computation.5 | async-start | bytes 6291456 | tf_op jit(solution)/shard_map/all_gather | solution.py:76
  252.9 108.3 %all-gather.5.cloned.1.call-start = ((), (), s32[]{:S(2)}) async-start(), calls=%async_computation.6 | async-start | bytes 3145728 | tf_op jit(solution)/shard_map/all_gather | solution.py:77
  309.9 10.0 %copy-start = (f32[1024,1024]{1,0:T(8,128)S(1)}, f32[1024,1024]{1,0:T(8,128)}, u32[]{:S(2)}) copy-start(f32[1024,1024]{1,0:T(8,128)} %get-tuple-element.5) | copy-start | bytes 12582916
  319.9 8.1 %copy-start.2 = (s32[352,1]{0,1:T(1,128)S(1)}, s32[352,1]{0,1:T(1,128)}, u32[]{:S(2)}) copy-start(s32[352,1]{0,1:T(1,128)} %param.4) | copy-start | bytes 4228
  319.9 41.4 %copy-start.1 = (bf16[352,1024]{1,0:T(8,128)(2,1)S(1)}, bf16[352,1024]{1,0:T(8,128)(2,1)}, u32[]{:S(2)}) copy-start(bf16[352,1024]{1,0:T(8,128)(2,1)} %param.3) | copy-start | bytes 2162692
  332.8 34.8 %all-to-all-start.1 = ((bf16[16,1,64]{2,1,0:T(2,128)(2,1)}), bf16[16,1,64]{2,1,0:T(2,128)(2,1)S(1)}, u32[]{:S(2)}, u32[]{:S(2)}) async-start(bf16[16,1,64]{2,1,0:T(2,128)(2,1)} %all_to_all.16), calls=%async_computation.1 | async-start | bytes 16384 | tf_op jit(solution)/shard_map/all_to_all | solution.py:92
  367.6 53.8 %all-to-all-start = ((bf16[16,64,1024]{2,1,0:T(8,128)(2,1)}), bf16[16,64,1024]{2,1,0:T(8,128)(2,1)S(1)}, u32[]{:S(2)}, u32[]{:S(2)}) async-start(bf16[16,64,1024]{2,1,0:T(8,128)(2,1)} %bitcast.2), calls=%async_computation | async-start | bytes 4194304 | tf_op jit(solution)/shard_map/all_to_all | solution.py:85
  428.6 52.3 %all-to-all-start.2 = ((bf16[16,64,1024]{2,1,0:T(8,128)(2,1)}), bf16[16,64,1024]{2,1,0:T(8,128)(2,1)S(1)}, u32[]{:S(2)}, u32[]{:S(2)}) async-start(bf16[16,64,1024]{2,1,0:T(8,128)(2,1)} %bitcast.30), calls=%async_computation.2 | async-start | bytes 4194304 | tf_op jit(solution)/shard_map/all_to_all | solution.py:103
Sparse Core Ops, SparseCore 0:
  12.1 108.9 all-reduce.3
  125.3 110.2 all-reduce.5
  253.1 56.7 all-gather.2
  328.1 33.1 all-gather.4
